TPU v7x, 32 devices: a whole 2x2x4 slice. The times are simulated.
32 devices in a mesh: pipe: 4 (over x, core), dp: 2 (over y), vocab: 4 (over z).
Axes of the slice: x: 2, y: 2, z: 4, core: 2. Of those that a mesh axis runs over, the one named last changes fastest.
Arguments:
- hidden: bfloat16 [512, 4608], P(('pipe', 'dp', 'vocab')), may hold values from -6 to 6
- targets: int32 [512], P(('pipe', 'dp', 'vocab')), may hold values from 0 to 12287, as said below
- input_ids: int32 [512], P(('pipe', 'dp', 'vocab')), may hold values from 0 to 12287, as said below
- input_grads: bfloat16 [512, 4608], P(('pipe', 'dp', 'vocab')), may hold values from -0.3125 to 0.3125
- table: bfloat16 [12288, 4608], P(('pipe', 'vocab'), 'dp'), may hold values from -0.75 to 0.75
- keep: int32 [12288], P(('pipe', 'vocab')), may hold values from 0 to 1
- first_moment: bfloat16 [12288, 4608], P(('pipe', 'vocab'), 'dp'), may hold values from -0.015625 to 0.015625
- second_moment: bfloat16 [12288, 4608], P(('pipe', 'vocab'), 'dp'), may hold values from 9.983778e-07 to 9.953976e-06
Outputs:
- new_table: bfloat16 [12288, 4608], P(('pipe', 'vocab'), 'dp')
- new_first: bfloat16 [12288, 4608], P(('pipe', 'vocab'), 'dp')
- new_second: bfloat16 [12288, 4608], P(('pipe', 'vocab'), 'dp')
- loss: float32 [], replicated
Inputs may be any that keep to these rules, and one draw needn't show every extreme that they name: `targets`: names only rows with keep = 1. `input_ids`: names only rows with keep = 1.
All inputs are finite; a program needn't handle non-finite values.
Results may differ from a plain program's by a relative error of at most 0.0036.
Values may be sent and summed in bfloat16 or wider, within the bound.
A program may use at most 192 MiB of HBM per device.

v0:
```python
import math
import jax
import jax.numpy as jnp
from jax import lax
from jax.sharding import PartitionSpec as P

SOFTCAP = 30.0
LEARN = 0.01
EPSILON = 1e-08


def contract_last(left, right):
    return lax.dot_general(
        left, right, (((1,), (1,)), ((), ())), preferred_element_type=jnp.float32
    )


def contract_first(left, right):
    return lax.dot_general(
        left, right, (((0,), (0,)), ((), ())), preferred_element_type=jnp.float32
    )


def body(hidden, targets, input_ids, input_grads, table, keep, first_moment, second_moment):
    rows_here = table.shape[0]
    row_start = lax.axis_index(("pipe", "vocab")) * rows_here
    keepf = keep.astype(jnp.float32)
    scale = math.sqrt(hidden.shape[1])
    groups_dp = lax.axis_size("dp")
    row_iota = jnp.arange(rows_here, dtype=jnp.int32)
    both = jnp.stack([targets, input_ids])
    packed = lax.all_to_all(
        jnp.stack([hidden, input_grads]), "dp", split_axis=2, concat_axis=1, tiled=True
    )
    ids_all = lax.all_gather(both, ("pipe", "vocab", "dp"), axis=1, tiled=True)
    tokens_all = lax.all_gather(packed[0], ("pipe", "vocab"), axis=0, tiled=True)
    grads_all = lax.all_gather(packed[1], ("pipe", "vocab"), axis=0, tiled=True)
    tokens = tokens_all.shape[0]
    share = tokens // groups_dp
    start = lax.axis_index("dp") * share
    goals = lax.dynamic_slice(ids_all[0], (start,), (share,))
    raw = lax.psum_scatter(contract_last(tokens_all, table), "dp", scatter_dimension=0, tiled=True)
    capped = SOFTCAP * jnp.tanh(raw / SOFTCAP)
    onehot = ((goals - row_start)[:, None] == row_iota[None, :]).astype(jnp.float32)
    weights = jnp.exp(capped) * keepf[None, :]
    local = jnp.stack([jnp.sum(weights, axis=1), jnp.sum(capped * onehot, axis=1)])
    placed = lax.dynamic_update_slice(jnp.zeros((2, tokens), jnp.float32), local, (0, start))
    sums = lax.psum(placed, ("pipe", "dp", "vocab"))
    token_loss = jnp.sum(jnp.log(sums[0]) - sums[1])
    total = lax.dynamic_slice(sums[0], (start,), (share,))
    slope = 1.0 - (capped / SOFTCAP) ** 2
    dlogits = ((weights / total[:, None] - onehot) * slope).astype(jnp.bfloat16)
    dlogits = lax.all_gather(dlogits, "dp", axis=0, tiled=True)
    selector = ((ids_all[1] - row_start)[None, :] == row_iota[:, None]).astype(jnp.bfloat16)
    finished = contract_first(dlogits, tokens_all) + scale * jnp.dot(
        selector, grads_all, preferred_element_type=jnp.float32
    )
    kept = keep[:, None] > 0
    first_new = (0.9 * first_moment.astype(jnp.float32) + 0.1 * finished).astype(jnp.bfloat16)
    second_new = (0.95 * second_moment.astype(jnp.float32) + 0.05 * finished * finished).astype(
        jnp.bfloat16
    )
    corr_one = 1.0 - 0.9**10
    corr_two = 1.0 - 0.95**10
    update = (
        first_new.astype(jnp.float32)
        / corr_one
        / (jnp.sqrt(second_new.astype(jnp.float32) / corr_two) + EPSILON)
    )
    table_new = (table.astype(jnp.float32) - LEARN * update).astype(jnp.bfloat16)
    new_table = jnp.where(kept, table_new, table)
    new_first = jnp.where(kept, first_new, first_moment)
    new_second = jnp.where(kept, second_new, second_moment)
    return (new_table, new_first, new_second, token_loss)


def solution(mesh):
    placed = (
        P(("pipe", "dp", "vocab"), None),
        P(("pipe", "dp", "vocab")),
        P(("pipe", "dp", "vocab")),
        P(("pipe", "dp", "vocab"), None),
        P(("pipe", "vocab"), "dp"),
        P(("pipe", "vocab")),
        P(("pipe", "vocab"), "dp"),
        P(("pipe", "vocab"), "dp"),
    )
    return jax.shard_map(
        body,
        mesh=mesh,
        in_specs=placed,
        out_specs=(
            P(("pipe", "vocab"), "dp"),
            P(("pipe", "vocab"), "dp"),
            P(("pipe", "vocab"), "dp"),
            P(),
        ),
        check_vma=False,
    )
```

profile of v0, /device:TPU:10, one launch (start us, length us, event | category | flops | bytes accessed | tf_op | source)
XLA Modules:
  0.0 227.2 jit_solution(489731304706484116)
XLA Ops:
  7.2 0.0 all-gather.4.cloned.1.call-start
  7.2 1.0 pad_maximum_fusion
  8.2 3.0 %copy.27 = bf16[2,16,4608]{1,0,2:T(2,128)(2,1)S(1)} copy(bf16[2,16,4608]{2,1,0:T(8,128)(2,1)S(1)} %pad_maximum_fusion) | data formatting | bytes 589824 | tf_op jit(solution)/shard_map/stack | solution.py:33
  11.2 2.5 %reshape.30 = bf16[2,2,36864]{2,1,0:T(2,128)(2,1)S(1)} reshape(bf16[4608,2,16]{2,1,0:T(2,128)(2,1)S(1)} %bitcast.27) | data formatting | bytes 589824
  13.7 8.2 %all_to_all.15 = bf16[2,2,36864]{2,1,0:T(2,128)(2,1)S(1)} all-to-all(bf16[2,2,36864]{2,1,0:T(2,128)(2,1)S(1)} %reshape.30), channel_id=1, replica_groups=mesh['pipe'=4,'dp'=2,'vocab'=4] {'dp'}, dimensions={0} | all-to-all | bytes 589824 | tf_op jit(solution)/shard_map/all_to_all | solution.py:32
  21.9 1.6 reshape.31
  23.5 1.6 copy.32
  25.1 0.2 fusion.6
  25.3 0.7 copy.29
  26.0 0.0 all-gather.4.cloned.1.call-update
  26.0 0.0 copy-start.1
  26.0 0.0 copy-start.2
  26.0 0.0 copy-start.3
  26.1 0.0 reduce-scatter.2.cloned.1.call-start
  26.1 41.0 %all-gather.4.cloned.1.call-done = bf16[512,2304]{1,0:T(8,128)(2,1)} async-done(((bf16[32,2304]{1,0:T(8,128)(2,1)}), bf16[512,2304]{1,0:T(8,128)(2,1)}) %all-gather.4.cloned.1.call-update) | async-done | bytes 2359312 | tf_op jit(solution)/shard_map/all_gather | solution.py:36
  67.2 5.9 %fusion.7 = f32[512,768]{1,0:T(8,128)} fusion(bf16[512,2304]{1,0:T(8,128)(2,1)} %all-gather.4.cloned.1.call-done, bf16[768,2304]{1,0:T(8,128)(2,1)} %param.12), kind=kOutput, calls=%fused_computation.27 | convolution fusion | flops 1811939328 | bytes 7471104 | tf_op jit(solution)/shard_map/dot_general | solution.py:13
  73.0 0.0 copy-start
  73.0 0.0 reduce-scatter.2.cloned.1.call-update
  73.1 0.0 all-gather.6.cloned.1.call-start
  73.1 0.7 copy.31
  73.8 0.0 all-gather.6.cloned.1.call-update
  73.8 0.0 copy-done.1
  73.8 0.0 copy-done.2
  73.9 0.0 copy-done.3
  73.9 65.0 %all-gather = s32[32,16,2]{1,2,0:T(2,128)S(1)} all-gather(s32[1,16,2]{1,2,0:T(2,128)S(1)} %add_bitcast_fusion), channel_id=1, replica_groups=mesh['pipe'=4,'dp'=2,'vocab'=4] {'pipe','vocab','dp'}, dimensions={0}, use_global_device_ids=true | all-gather | bytes 4224 | tf_op jit(solution)/shard_map/all_gather | solution.py:35
  138.8 0.1 reshape.29
  139.0 0.0 reduce-scatter.2.cloned.1.call-done
  139.0 1.6 fusion.4
  140.7 42.0 %psum.7 = f32[2,512]{1,0:T(2,128)S(1)} all-reduce(f32[2,512]{1,0:T(2,128)S(1)} %maximum_dynamic-update-slice_fusion), channel_id=1, replica_groups=mesh['pipe'=4,'dp'=2,'vocab'=4] {'pipe','dp','vocab'}, use_global_device_ids=true, to_apply=%region_3.0 | all-reduce | flops 1024 | bytes 8192 | tf_op jit(solution)/shard_map/psum | solution.py:48
  182.6 0.6 fusion.5
  183.2 1.5 multiply_convert_fusion
  184.8 10.6 %all_gather.14 = bf16[512,768]{1,0:T(8,128)(2,1)S(1)} all-gather(bf16[256,768]{1,0:T(8,128)(2,1)S(1)} %multiply_convert_fusion), channel_id=1, replica_groups=mesh['pipe'=4,'dp'=2,'vocab'=4] {'dp'}, dimensions={0}, use_global_device_ids=true | all-gather | bytes 1179648 | tf_op jit(solution)/shard_map/all_gather | solution.py:53
  195.4 0.0 copy-done
  195.4 5.0 %fusion.8 = f32[768,2304]{1,0:T(8,128)} fusion(bf16[512,768]{1,0:T(8,128)(2,1)S(1)} %all_gather.14, bf16[512,2304]{1,0:T(8,128)(2,1)S(1)} %copy-done), kind=kOutput, calls=%fused_computation.28 | convolution fusion | flops 1811939328 | bytes 10223616 | tf_op jit(solution)/shard_map/dot_general | solution.py:19
  200.4 0.0 all-gather.6.cloned.1.call-done
  200.4 20.3 %broadcast_select_fusion = (bf16[768,2304]{1,0:T(8,128)(2,1)}, bf16[768,2304]{1,0:T(8,128)(2,1)}, bf16[768,2304]{1,0:T(8,128)(2,1)}) fusion(bf16[768,2304]{1,0:T(8,128)(2,1)} %param.15, pred[768]{0:T(1024)(128)(4,1)S(1)} %broadcast_compare_fusion, bf16[768,2304]{1,0:T(8,128)(2,1)} %param.12, bf16[768,2304]{1,0:T(8,128)(2,1)} %param.14, ...), kind=kOutput, calls=%fused_computation.7 | convolution fusion | flops 1858338816 | bytes 30673664 | tf_op jit(solution)/shard_map/dot_general | solution.py:55
  (9 shorter events, 0.1 us)
Async XLA Ops:
  7.2 60.0 %all-gather.4.cloned.1.call-start = ((), (), s32[]{:S(2)}) async-start(), calls=%async_computation.2 | async-start | bytes 2506752 | tf_op jit(solution)/shard_map/all_gather | solution.py:36
  26.0 47.8 %copy-start.1 = (s32[768]{0:T(1024)S(1)}, s32[768]{0:T(1024)}, u32[]{:S(2)}) copy-start(s32[768]{0:T(1024)} %param.13) | copy-start | bytes 9220
  26.0 47.8 %copy-start.2 = (s32[16]{0:T(128)S(1)}, s32[16]{0:T(128)}, u32[]{:S(2)}) copy-start(s32[16]{0:T(128)} %param.10) | copy-start | bytes 196
  26.0 47.8 %copy-start.3 = (s32[16]{0:T(128)S(1)}, s32[16]{0:T(128)}, u32[]{:S(2)}) copy-start(s32[16]{0:T(128)} %param.9) | copy-start | bytes 196
  26.1 113.0 %reduce-scatter.2.cloned.1.call-start = ((), (), s32[]{:S(2)}) async-start(), calls=%async_computation.3 | async-start | bytes 2359296 | tf_op jit(solution)/shard_map/reduce_scatter | solution.py:42
  73.0 122.4 %copy-start = (bf16[512,2304]{1,0:T(8,128)(2,1)S(1)}, bf16[512,2304]{1,0:T(8,128)(2,1)}, u32[]{:S(2)}) copy-start(bf16[512,2304]{1,0:T(8,128)(2,1)} %all-gather.4.cloned.1.call-done) | copy-start | bytes 7077892
  73.1 127.3 %all-gather.6.cloned.1.call-start = ((), (), s32[]{:S(2)}) async-start(), calls=%async_computation.4 | async-start | bytes 2506752 | tf_op jit(solution)/shard_map/all_gather | solution.py:37
Sparse Core Ops, SparseCore 0:
  26.1 40.9 all-gather.3
  73.2 26.5 reduce-scatter.1
  102.9 40.8 all-gather.5
where the time goes:
time: 228 us; the launch traced here: 227 us
  blocking collectives  126 us (55%)
  waiting for transfers between devices  41.1 us (18%)
  matrix products  31.1 us (14%)
  between operations  13.9 us (6%)
  local copies, waits for them, and re-layouts  10.4 us (5%)
  other arithmetic  4.81 us (2%)
    all_gather x1, blocking collectives, body(): ids_all = lax.all_gather(both, ('pipe', 'vocab', 'dp'), axis=1, tiled=True)  65 us
    psum x1, blocking collectives, body(): sums = lax.psum(placed, ('pipe', 'dp', 'vocab'))  42 us
    all_gather x1, waiting for transfers between devices, body(): lax.all_gather(packed[0], ('pipe', 'vocab'), axis=0, tiled=True)  41 us
    dot_general x1, matrix products, body(): jnp.dot(selector, grads_all, preferred_element_type=jnp.float32)  20.3 us
    all_gather x1, blocking collectives, body(): dlogits = lax.all_gather(dlogits, 'dp', axis=0, tiled=True)  10.6 us
    all_to_all x1, blocking collectives, body(): lax.all_to_all(jnp.stack([hidden, input_grads]), 'dp', split_axis=2, conc...  8.17 us
    dot_general x1, matrix products, contract_last(): lax.dot_general(left, right, (((1,), (1,)), ((), ())), preferred_element_...  5.88 us
    dot_general x1, matrix products, contract_first(): lax.dot_general(left, right, (((0,), (0,)), ((), ())), preferred_element_...  4.95 us
  transfers between devices with their start and end apart: 3, of which 1 were waited for; matrix products, arithmetic and copies ran while one was open for 4% of the time, Pallas kernels for 0%

commit v1 on v0

--- a/solution.py
+++ b/solution.py
@@ -45,7 +45,7 @@
     weights = jnp.exp(capped) * keepf[None, :]
     local = jnp.stack([jnp.sum(weights, axis=1), jnp.sum(capped * onehot, axis=1)])
     placed = lax.dynamic_update_slice(jnp.zeros((2, tokens), jnp.float32), local, (0, start))
-    sums = lax.psum(placed, ("pipe", "dp", "vocab"))
+    sums = lax.psum(lax.psum(placed, ("dp", "vocab")), "pipe")
     token_loss = jnp.sum(jnp.log(sums[0]) - sums[1])
     total = lax.dynamic_slice(sums[0], (start,), (share,))
     slope = 1.0 - (capped / SOFTCAP) ** 2

time: 228 us -> 214 us (0.939)
  blocking collectives: 126 us -> 111 us
    psum x1 -> x2, blocking collectives: 42 us -> 26.1 us  [body(): sums = lax.psum(lax.psum(placed, ('dp', 'vocab')), 'pipe')]
where the time goes in v1:
time: 214 us; the launch traced here: 212 us
  blocking collectives  111 us (52%)
  waiting for transfers between devices  41.1 us (19%)
  matrix products  31.1 us (15%)
  between operations  13.9 us (6%)
  local copies, waits for them, and re-layouts  10.4 us (5%)
  other arithmetic  4.82 us (2%)
    all_gather x1, blocking collectives, body(): ids_all = lax.all_gather(both, ('pipe', 'vocab', 'dp'), axis=1, tiled=True)  65 us
    all_gather x1, waiting for transfers between devices, body(): lax.all_gather(packed[0], ('pipe', 'vocab'), axis=0, tiled=True)  41 us
    psum x2, blocking collectives, body(): sums = lax.psum(lax.psum(placed, ('dp', 'vocab')), 'pipe')  26.1 us
    dot_general x1, matrix products, body(): jnp.dot(selector, grads_all, preferred_element_type=jnp.float32)  20.3 us
    all_gather x1, blocking collectives, body(): dlogits = lax.all_gather(dlogits, 'dp', axis=0, tiled=True)  11.6 us
    all_to_all x1, blocking collectives, body(): lax.all_to_all(jnp.stack([hidden, input_grads]), 'dp', split_axis=2, conc...  8.17 us
    dot_general x1, matrix products, contract_last(): lax.dot_general(left, right, (((1,), (1,)), ((), ())), preferred_element_...  5.88 us
    dot_general x1, matrix products, contract_first(): lax.dot_general(left, right, (((0,), (0,)), ((), ())), preferred_element_...  4.95 us
  transfers between devices with their start and end apart: 3, of which 1 were waited for; matrix products, arithmetic and copies ran while one was open for 4% of the time, Pallas kernels for 0%

profile of v1, /device:TPU:10, one launch (start us, length us, event | category | flops | bytes accessed | tf_op | source)
XLA Modules:
  0.0 212.3 jit_solution(16045910925544246098)
XLA Ops:
  7.2 0.0 all-gather.4.cloned.1.call-start
  7.2 1.0 pad_maximum_fusion
  8.2 3.0 %copy.27 = bf16[2,16,4608]{1,0,2:T(2,128)(2,1)S(1)} copy(bf16[2,16,4608]{2,1,0:T(8,128)(2,1)S(1)} %pad_maximum_fusion) | data formatting | bytes 589824 | tf_op jit(solution)/shard_map/stack | solution.py:33
  11.2 2.5 %reshape.30 = bf16[2,2,36864]{2,1,0:T(2,128)(2,1)S(1)} reshape(bf16[4608,2,16]{2,1,0:T(2,128)(2,1)S(1)} %bitcast.27) | data formatting | bytes 589824
  13.7 8.2 %all_to_all.15 = bf16[2,2,36864]{2,1,0:T(2,128)(2,1)S(1)} all-to-all(bf16[2,2,36864]{2,1,0:T(2,128)(2,1)S(1)} %reshape.30), channel_id=1, replica_groups=mesh['pipe'=4,'dp'=2,'vocab'=4] {'dp'}, dimensions={0} | all-to-all | bytes 589824 | tf_op jit(solution)/shard_map/all_to_all | solution.py:32
  21.9 1.6 reshape.31
  23.5 1.6 copy.32
  25.1 0.2 fusion.6
  25.3 0.7 copy.29
  26.0 0.0 all-gather.4.cloned.1.call-update
  26.0 0.0 copy-start.1
  26.0 0.0 copy-start.2
  26.0 0.0 copy-start.3
  26.1 0.0 reduce-scatter.2.cloned.1.call-start
  26.1 41.0 %all-gather.4.cloned.1.call-done = bf16[512,2304]{1,0:T(8,128)(2,1)} async-done(((bf16[32,2304]{1,0:T(8,128)(2,1)}), bf16[512,2304]{1,0:T(8,128)(2,1)}) %all-gather.4.cloned.1.call-update) | async-done | bytes 2359312 | tf_op jit(solution)/shard_map/all_gather | solution.py:36
  67.2 5.9 %fusion.7 = f32[512,768]{1,0:T(8,128)} fusion(bf16[512,2304]{1,0:T(8,128)(2,1)} %all-gather.4.cloned.1.call-done, bf16[768,2304]{1,0:T(8,128)(2,1)} %param.12), kind=kOutput, calls=%fused_computation.27 | convolution fusion | flops 1811939328 | bytes 7471104 | tf_op jit(solution)/shard_map/dot_general | solution.py:13
  73.0 0.0 copy-start
  73.0 0.0 reduce-scatter.2.cloned.1.call-update
  73.1 0.0 all-gather.6.cloned.1.call-start
  73.1 0.7 copy.31
  73.8 0.0 all-gather.6.cloned.1.call-update
  73.8 0.0 copy-done.1
  73.8 0.0 copy-done.2
  73.9 0.0 copy-done.3
  73.9 65.0 %all-gather = s32[32,16,2]{1,2,0:T(2,128)S(1)} all-gather(s32[1,16,2]{1,2,0:T(2,128)S(1)} %add_bitcast_fusion), channel_id=1, replica_groups=mesh['pipe'=4,'dp'=2,'vocab'=4] {'pipe','vocab','dp'}, dimensions={0}, use_global_device_ids=true | all-gather | bytes 4224 | tf_op jit(solution)/shard_map/all_gather | solution.py:35
  138.8 0.1 reshape.29
  139.0 0.0 reduce-scatter.2.cloned.1.call-done
  139.0 1.6 fusion.4
  140.7 20.5 %psum.14 = f32[2,512]{1,0:T(2,128)S(1)} all-reduce(f32[2,512]{1,0:T(2,128)S(1)} %maximum_dynamic-update-slice_fusion), channel_id=1, replica_groups=mesh['pipe'=4,'dp'=2,'vocab'=4] {'dp','vocab'}, use_global_device_ids=true, to_apply=%region_3.0 | all-reduce | flops 1024 | bytes 8192 | tf_op jit(solution)/shard_map/psum | solution.py:48
  161.1 5.7 %psum.15 = f32[2,512]{1,0:T(2,128)S(1)} all-reduce(f32[2,512]{1,0:T(2,128)S(1)} %psum.14), channel_id=1, replica_groups=mesh['pipe'=4,'dp'=2,'vocab'=4] {'pipe'}, use_global_device_ids=true, to_apply=%region_4.0 | all-reduce | flops 1024 | bytes 8192 | tf_op jit(solution)/shard_map/psum | solution.py:48
  166.8 0.6 fusion.5
  167.4 1.5 multiply_convert_fusion
  169.0 11.6 %all_gather.14 = bf16[512,768]{1,0:T(8,128)(2,1)S(1)} all-gather(bf16[256,768]{1,0:T(8,128)(2,1)S(1)} %multiply_convert_fusion), channel_id=1, replica_groups=mesh['pipe'=4,'dp'=2,'vocab'=4] {'dp'}, dimensions={0}, use_global_device_ids=true | all-gather | bytes 1179648 | tf_op jit(solution)/shard_map/all_gather | solution.py:53
  180.5 0.0 copy-done
  180.5 4.9 %fusion.8 = f32[768,2304]{1,0:T(8,128)} fusion(bf16[512,768]{1,0:T(8,128)(2,1)S(1)} %all_gather.14, bf16[512,2304]{1,0:T(8,128)(2,1)S(1)} %copy-done), kind=kOutput, calls=%fused_computation.28 | convolution fusion | flops 1811939328 | bytes 10223616 | tf_op jit(solution)/shard_map/dot_general | solution.py:19
  185.5 0.0 all-gather.6.cloned.1.call-done
  185.5 20.3 %broadcast_select_fusion = (bf16[768,2304]{1,0:T(8,128)(2,1)}, bf16[768,2304]{1,0:T(8,128)(2,1)}, bf16[768,2304]{1,0:T(8,128)(2,1)}) fusion(bf16[768,2304]{1,0:T(8,128)(2,1)} %param.15, pred[768]{0:T(1024)(128)(4,1)S(1)} %broadcast_compare_fusion, bf16[768,2304]{1,0:T(8,128)(2,1)} %param.12, bf16[768,2304]{1,0:T(8,128)(2,1)} %param.14, ...), kind=kOutput, calls=%fused_computation.7 | convolution fusion | flops 1858338816 | bytes 30673664 | tf_op jit(solution)/shard_map/dot_general | solution.py:55
  (9 shorter events, 0.1 us)
Async XLA Ops:
  7.2 60.0 %all-gather.4.cloned.1.call-start = ((), (), s32[]{:S(2)}) async-start(), calls=%async_computation.2 | async-start | bytes 2506752 | tf_op jit(solution)/shard_map/all_gather | solution.py:36
  26.0 47.8 %copy-start.1 = (s32[768]{0:T(1024)S(1)}, s32[768]{0:T(1024)}, u32[]{:S(2)}) copy-start(s32[768]{0:T(1024)} %param.13) | copy-start | bytes 9220
  26.0 47.8 %copy-start.2 = (s32[16]{0:T(128)S(1)}, s32[16]{0:T(128)}, u32[]{:S(2)}) copy-start(s32[16]{0:T(128)} %param.10) | copy-start | bytes 196
  26.0 47.8 %copy-start.3 = (s32[16]{0:T(128)S(1)}, s32[16]{0:T(128)}, u32[]{:S(2)}) copy-start(s32[16]{0:T(128)} %param.9) | copy-start | bytes 196
  26.1 113.0 %reduce-scatter.2.cloned.1.call-start = ((), (), s32[]{:S(2)}) async-start(), calls=%async_computation.3 | async-start | bytes 2359296 | tf_op jit(solution)/shard_map/reduce_scatter | solution.py:42
  73.0 107.5 %copy-start = (bf16[512,2304]{1,0:T(8,128)(2,1)S(1)}, bf16[512,2304]{1,0:T(8,128)(2,1)}, u32[]{:S(2)}) copy-start(bf16[512,2304]{1,0:T(8,128)(2,1)} %all-gather.4.cloned.1.call-done) | copy-start | bytes 7077892
  73.1 112.4 %all-gather.6.cloned.1.call-start = ((), (), s32[]{:S(2)}) async-start(), calls=%async_computation.4 | async-start | bytes 2506752 | tf_op jit(solution)/shard_map/all_gather | solution.py:37
Sparse Core Ops, SparseCore 0:
  26.1 40.9 all-gather.3
  73.2 26.5 reduce-scatter.1
  102.9 40.9 all-gather.5
